TPU v7x, 512 devices: a whole 4x8x8 slice. The times are simulated.
512 devices in a mesh: lat: 128 (over x, z, y_hi), ch: 4 (over y_lo, core).
Axes of the slice: x: 4, y: 8 (y_hi: 4, y_lo: 2; y = y_hi * 2 + y_lo), z: 8, core: 2. Of those that a mesh axis runs over, the one named last changes fastest.
Arguments:
- tokens: bfloat16 [1, 256, 8, 69120], P(None, 'lat', 'ch'), may hold values from -6 to 6
- cotangent: bfloat16 [1, 256, 8, 69120], P(None, 'lat', 'ch'), may hold values from -6 to 6
- first_weight: bfloat16 [2, 8, 96, 96], P(None, 'ch'), may hold values from -0.4375 to 0.4375
- first_bias: bfloat16 [2, 8, 96], P(None, 'ch'), may hold values from -6 to 6
- second_weight: bfloat16 [2, 8, 96, 96], P(None, 'ch'), may hold values from -0.4375 to 0.4375
- relu_mask: int32 [1, 2, 8, 256, 24576], P(None, None, 'ch', 'lat'), may hold values 0 or 1
- shrink_mask: int32 [1, 2, 8, 256, 24576], P(None, None, 'ch', 'lat'), may hold values 0 or 1
Outputs:
- token_gradient: bfloat16 [1, 256, 8, 69120], P(None, 'lat', 'ch')
- first_gradient: float32 [2, 8, 96, 96], P(None, 'ch')
- bias_gradient: float32 [2, 8, 96], P(None, 'ch')
- second_gradient: float32 [2, 8, 96, 96], P(None, 'ch')
All inputs are finite; a program needn't handle non-finite values. No bound on the sum of `relu_mask` or of `shrink_mask` on one device may be relied on, other than what follows from the above.
Results may differ from a plain program's by a relative error of at most 0.0093.
Values may be sent and summed in bfloat16 or wider, within the bound.
A program may use at most 64 MiB of HBM per device.

v0:
```python
import math

import jax
import jax.numpy as jnp
from jax import lax
from jax.sharding import Mesh
from jax.sharding import PartitionSpec as P

WAVES = 256
LAT = ("lat_0", "lat_1", "lat_2")


def side_by_side(arrays, axis, split_dim, concat_dim, along):
    ends, at = ([], 0)
    for a in arrays[:-1]:
        at += a.shape[along]
        ends.append(at)
    both = jnp.concatenate(arrays, axis=along)
    return tuple(
        jnp.split(
            lax.all_to_all(both, axis, split_axis=split_dim, concat_axis=concat_dim, tiled=True),
            ends,
            axis=along,
        )
    )


def in_blocks(shard, dim, devices):
    before, after = (shard.shape[:dim], shard.shape[dim + 1 :])
    return jnp.moveaxis(shard.reshape(*before, devices, -1, *after), dim, 0)


def summed_on_arrival(shard, axis, dim):
    parts = in_blocks(shard, dim, lax.axis_size(axis))
    arrived = lax.all_to_all(parts, axis, split_axis=0, concat_axis=0, tiled=True)
    return arrived.sum(axis=0)


def sum_by_axis(shard, axes, dim):
    far, near = axes
    own = summed_on_arrival(in_blocks(shard, dim, lax.axis_size(far)), near, dim + 1)
    return jnp.sum(lax.all_to_all(own, far, 0, 0, tiled=True), axis=0)


def filled_up(lines, devices):
    spare = -lines.shape[0] % devices
    if not spare:
        return lines
    return jnp.concatenate([lines, jnp.zeros((spare, *lines.shape[1:]), lines.dtype)])


def sent_to_all(shard, axis):
    devices = lax.axis_size(axis)
    return lax.all_to_all(
        jnp.broadcast_to(shard[None], (devices, *shard.shape)), axis, 0, 0, tiled=True
    )


def laid_out(parts, dim):
    parts = jnp.moveaxis(parts, 0, dim)
    lengths = parts.shape
    return parts.reshape(*lengths[:dim], lengths[dim] * lengths[dim + 1], *lengths[dim + 2 :])


def whole_of(shard, axes, dim):
    far, near = axes
    leading = sent_to_all(shard, far)
    parts = jnp.swapaxes(sent_to_all(leading, near), 0, 1)
    return laid_out(parts.reshape(-1, *shard.shape), dim)


def sum_by_parts(shard, axes):
    own = sum_by_axis(filled_up(shard, lax.axis_size(axes[0]) * lax.axis_size(axes[1])), axes, 0)
    whole = whole_of(own, axes, 0)
    return whole[: len(shard)].reshape(shard.shape)


def packed_total(arrays, axis):
    ravelled, at, done = (jnp.concatenate([a.reshape(-1) for a in arrays]), 0, [])
    so_far = sum_by_parts(ravelled, axis)
    for a in arrays:
        done.append(so_far[at : at + a.size].reshape(a.shape))
        at += a.size
    return tuple(done)


def east_basis(count, waves):
    column = jnp.arange(count, dtype=jnp.int32)[:, None]
    number = jnp.arange(waves, dtype=jnp.int32)[None, :]
    phase = (column * number % count).astype(jnp.float32) * (2.0 * math.pi / count)
    factor = 1.0 / math.sqrt(count)
    return jnp.stack([jnp.cos(phase) * factor, -jnp.sin(phase) * factor], axis=1)


def north_basis(count):
    column = jnp.arange(count, dtype=jnp.int32)[:, None]
    number = jnp.arange(count, dtype=jnp.int32)[None, :]
    phase = (column * number % count).astype(jnp.float32) * (2.0 * math.pi / count)
    factor = 1.0 / math.sqrt(count)
    cosine = jnp.cos(phase) * factor
    sine = jnp.sin(phase) * factor
    upper = jnp.concatenate([cosine, sine], axis=1)
    lower = jnp.concatenate([-sine, cosine], axis=1)
    return jnp.concatenate([upper, lower], axis=0)


def complex_mix(left_real, left_imag, right_real, right_imag, form):
    real_part = jnp.einsum(
        form, left_real, right_real, preferred_element_type=jnp.float32
    ) - jnp.einsum(form, left_imag, right_imag, preferred_element_type=jnp.float32)
    imag_part = jnp.einsum(
        form, left_real, right_imag, preferred_element_type=jnp.float32
    ) + jnp.einsum(form, left_imag, right_real, preferred_element_type=jnp.float32)
    return (real_part, imag_part)


def local(tokens, cotangent, first_weight, first_bias, second_weight, relu_mask, shrink_mask):
    batches, lat_rows, blocks_dev, flat_east = tokens.shape
    block_width = first_weight.shape[2]
    east_cells = flat_east // block_width
    east_table = east_basis(east_cells, WAVES).astype(jnp.bfloat16)

    def to_waves(field):
        grid = field.reshape(batches, lat_rows, blocks_dev, east_cells, block_width)
        return jnp.einsum(
            "bhnwe,wsk->bsnkhe", grid, east_table, preferred_element_type=jnp.float32
        ).astype(jnp.bfloat16)

    spec_tokens, spec_cotangent = side_by_side(
        (to_waves(tokens), to_waves(cotangent)), LAT, 3, 4, 0
    )
    wave_dev = spec_tokens.shape[3]
    north_cells = spec_tokens.shape[4]
    north_table = (
        north_basis(north_cells).astype(jnp.bfloat16).reshape(2, north_cells, 2, north_cells)
    )
    factor = 1.0 / math.sqrt(north_cells * WAVES)
    shape_modes = (batches, 2, blocks_dev, wave_dev, north_cells, block_width)

    def to_modes(spec):
        return jnp.einsum(
            "tqsp,bsnkpe->btnkqe", north_table, spec, preferred_element_type=jnp.float32
        ).astype(jnp.bfloat16)

    relu_keep = relu_mask.reshape(shape_modes).astype(jnp.float32)
    shrink_keep = shrink_mask.reshape(shape_modes).astype(jnp.bfloat16)
    modes = to_modes(spec_tokens)
    upstream = to_modes(spec_cotangent) * shrink_keep
    before_real, before_imag = complex_mix(
        modes[:, 0], modes[:, 1], first_weight[0], first_weight[1], "bnkqe,nef->bnkqf"
    )
    bias_real = first_bias[0].astype(jnp.float32)[None, :, None, None, :]
    bias_imag = first_bias[1].astype(jnp.float32)[None, :, None, None, :]
    hidden_real = (relu_keep[:, 0] * (before_real + bias_real)).astype(jnp.bfloat16)
    hidden_imag = (relu_keep[:, 1] * (before_imag + bias_imag)).astype(jnp.bfloat16)
    second_real, second_imag = complex_mix(
        hidden_real, -hidden_imag, upstream[:, 0], upstream[:, 1], "bnkqe,bnkqf->nef"
    )
    second_grad = jnp.stack([second_real, second_imag]) * factor
    back_real, back_imag = complex_mix(
        upstream[:, 0], upstream[:, 1], second_weight[0], -second_weight[1], "bnkqf,nef->bnkqe"
    )
    inner_real = (relu_keep[:, 0] * back_real).astype(jnp.bfloat16)
    inner_imag = (relu_keep[:, 1] * back_imag).astype(jnp.bfloat16)
    first_real, first_imag = complex_mix(
        modes[:, 0], -modes[:, 1], inner_real, inner_imag, "bnkqe,bnkqf->nef"
    )
    first_grad = jnp.stack([first_real, first_imag]) * factor
    bias_grad = (
        jnp.stack(
            [
                jnp.sum(inner_real.astype(jnp.float32), axis=(0, 2, 3)),
                jnp.sum(inner_imag.astype(jnp.float32), axis=(0, 2, 3)),
            ]
        )
        * factor
    )
    first_grad, bias_grad, second_grad = packed_total(
        (first_grad, bias_grad, second_grad), (("lat_0", "lat_1"), "lat_2")
    )
    mode_real, mode_imag = complex_mix(
        inner_real, inner_imag, first_weight[0], -first_weight[1], "bnkqf,nef->bnkqe"
    )
    stacked = jnp.stack([mode_real, mode_imag], axis=1).astype(jnp.bfloat16)
    returned = jnp.einsum(
        "tqsp,btnkqe->bsnkpe", north_table, stacked, preferred_element_type=jnp.float32
    ).astype(jnp.bfloat16)
    returned = lax.all_to_all(returned, LAT, split_axis=4, concat_axis=3, tiled=True)
    token_grad = jnp.einsum(
        "bsnkhe,wsk->bhnwe", returned, east_table, preferred_element_type=jnp.float32
    )
    token_grad = token_grad.reshape(batches, lat_rows, blocks_dev, flat_east)
    token_gradient = (token_grad + cotangent.astype(jnp.float32)).astype(jnp.bfloat16)
    return (token_gradient, first_grad, bias_grad, second_grad)


def solution(mesh):
    finer = Mesh(mesh.devices.reshape(4, 8, 4, mesh.shape["ch"]), ("lat_0", "lat_1", "lat_2", "ch"))
    in_specs = (
        P(None, LAT, "ch", None),
        P(None, LAT, "ch", None),
        P(None, "ch", None, None),
        P(None, "ch", None),
        P(None, "ch", None, None),
        P(None, None, "ch", LAT, None),
        P(None, None, "ch", LAT, None),
    )
    out_specs = (
        P(None, LAT, "ch", None),
        P(None, "ch", None, None),
        P(None, "ch", None),
        P(None, "ch", None, None),
    )
    return jax.shard_map(local, mesh=finer, in_specs=in_specs, out_specs=out_specs, check_vma=False)
```

profile of v0, /device:TPU:8, one launch (start us, length us, event | category | flops | bytes accessed | tf_op | source)
XLA Modules:
  0.0 161.7 jit_solution(14134927813874337274)
XLA Ops:
  0.6 3.3 %multiply_convert_fusion = (bf16[720,1,256]{2,0,1:T(8,128)(2,1)S(1)}, bf16[720,1,256]{2,0,1:T(8,128)(2,1)S(1)}) fusion(), kind=kLoop, calls=%fused_computation.71 | loop fusion | flops 2580480 | bytes 737280 | tf_op jit(solution)/shard_map/convert.17
  4.0 2.0 %reshape.282 = bf16[2,2,720,96]{3,2,1,0:T(8,128)(2,1)S(1)} reshape(bf16[1,2,2,69120]{3,2,1,0:T(2,128)(2,1)} %param.7) | data formatting | bytes 1105920 | tf_op jit(solution)/shard_map/reshape
  7.9 2.1 %copy.72 = bf16[2,2,2,256,2,96]{5,2,4,1,0,3:T(2,128)(2,1)} copy(bf16[2,2,2,256,2,96]{3,5,2,4,1,0:T(8,128)(2,1)S(1)} %pad_maximum_fusion) | data formatting | bytes 1572864 | tf_op jit(solution)/shard_map/concatenate | solution.py:18
  10.0 19.6 %all-to-all-start = ((bf16[2,2,2,256,2,96]{5,2,4,1,0,3:T(2,128)(2,1)}), bf16[2,2,2,256,2,96]{5,2,4,1,0,3:T(2,128)(2,1)S(1)}, u32[]{:S(2)}, u32[]{:S(2)}) async-start(bf16[2,2,2,256,2,96]{5,2,4,1,0,3:T(2,128)(2,1)} %copy.72), calls=%async_computation | async-start | bytes 2097152 | tf_op jit(solution)/shard_map/all_to_all | solution.py:21
  29.5 1.0 fusion.62
  30.5 1.1 negate_convert_fusion
  31.7 0.9 convert_element_type.162
  32.6 1.4 convert_element_type.166
  34.4 1.0 copy.77
  35.4 1.4 convert_element_type.153
  37.6 1.1 fusion.105
  38.6 1.2 copy.152
  39.8 1.2 copy.151
  41.1 17.7 %all-to-all-done = bf16[2,2,2,256,2,96]{5,2,4,1,0,3:T(2,128)(2,1)S(1)} async-done(((bf16[2,2,2,256,2,96]{5,2,4,1,0,3:T(2,128)(2,1)}), bf16[2,2,2,256,2,96]{5,2,4,1,0,3:T(2,128)(2,1)S(1)}, u32[]{:S(2)}, u32[]{:S(2)}) %all-to-all-start) | async-done | bytes 786464 | tf_op jit(solution)/shard_map/all_to_all | solution.py:21
  62.7 1.0 fusion.78
  64.0 0.8 convolution_bitcast_fusion.6
  69.0 6.4 %all-to-all-start.2 = ((f32[4,32,579]{2,1,0:T(8,128)}), f32[4,32,579]{2,1,0:T(8,128)S(1)}, u32[]{:S(2)}, u32[]{:S(2)}) async-start(f32[4,32,579]{2,1,0:T(8,128)} %copy.93), calls=%async_computation.2 | async-start | bytes 655360 | tf_op jit(solution)/shard_map/all_to_all | solution.py:35
  75.8 10.2 %all-to-all-done.2 = f32[4,32,579]{2,1,0:T(8,128)S(1)} async-done(((f32[4,32,579]{2,1,0:T(8,128)}), f32[4,32,579]{2,1,0:T(8,128)S(1)}, u32[]{:S(2)}, u32[]{:S(2)}) %all-to-all-start.2) | async-done | bytes 296480 | tf_op jit(solution)/shard_map/all_to_all | solution.py:35
  86.8 3.9 %all-to-all-start.3 = ((f32[32,1,579]{2,1,0:T(1,128)}), f32[32,1,579]{2,1,0:T(1,128)S(1)}, u32[]{:S(2)}, u32[]{:S(2)}) async-start(f32[32,1,579]{2,1,0:T(1,128)} %all_to_all.45), calls=%async_computation.3 | async-start | bytes 163840 | tf_op jit(solution)/shard_map/all_to_all | solution.py:42
  91.1 9.7 %all-to-all-done.3 = f32[32,1,579]{2,1,0:T(1,128)S(1)} async-done(((f32[32,1,579]{2,1,0:T(1,128)}), f32[32,1,579]{2,1,0:T(1,128)S(1)}, u32[]{:S(2)}, u32[]{:S(2)}) %all-to-all-start.3) | async-done | bytes 74144 | tf_op jit(solution)/shard_map/all_to_all | solution.py:42
  101.6 3.9 %all-to-all-start.4 = ((f32[32,1,579]{2,1,0:T(1,128)}), f32[32,1,579]{2,1,0:T(1,128)S(1)}, u32[]{:S(2)}, u32[]{:S(2)}) async-start(f32[32,1,579]{2,1,0:T(1,128)} %broadcast_in_dim.6), calls=%async_computation.4 | async-start | bytes 163840 | tf_op jit(solution)/shard_map/all_to_all | solution.py:54
  105.8 1.2 copy.81
  107.0 8.5 %all-to-all-done.4 = f32[32,1,579]{2,1,0:T(1,128)S(1)} async-done(((f32[32,1,579]{2,1,0:T(1,128)}), f32[32,1,579]{2,1,0:T(1,128)S(1)}, u32[]{:S(2)}, u32[]{:S(2)}) %all-to-all-start.4) | async-done | bytes 74144 | tf_op jit(solution)/shard_map/all_to_all | solution.py:54
  115.5 8.1 %all-to-all-start.1 = ((bf16[1,2,2,2,256,96]{5,1,3,2,0,4:T(2,128)(2,1)}), bf16[1,2,2,2,256,96]{5,1,3,2,0,4:T(2,128)(2,1)S(1)}, u32[]{:S(2)}, u32[]{:S(2)}) async-start(bf16[1,2,2,2,256,96]{5,1,3,2,0,4:T(2,128)(2,1)} %copy.81), calls=%async_computation.1 | async-start | bytes 1048576 | tf_op jit(solution)/shard_map/all_to_all | solution.py:188
  123.7 18.2 %all-to-all-done.1 = bf16[1,2,2,2,256,96]{5,1,3,2,0,4:T(2,128)(2,1)S(1)} async-done(((bf16[1,2,2,2,256,96]{5,1,3,2,0,4:T(2,128)(2,1)}), bf16[1,2,2,2,256,96]{5,1,3,2,0,4:T(2,128)(2,1)S(1)}, u32[]{:S(2)}, u32[]{:S(2)}) %all-to-all-start.1) | async-done | bytes 393248 | tf_op jit(solution)/shard_map/all_to_all | solution.py:188
  142.6 4.2 %all-to-all-start.5 = ((f32[4,32,579]{2,1,0:T(8,128)}), f32[4,32,579]{2,1,0:T(8,128)}, u32[]{:S(2)}, u32[]{:S(2)}) async-start(f32[4,32,579]{2,1,0:T(8,128)} %broadcast_in_dim.8), calls=%async_computation.5 | async-start | bytes 655360 | tf_op jit(solution)/shard_map/all_to_all | solution.py:54
  148.9 1.5 reshape.290
  150.3 1.4 add_convert_fusion
  151.7 5.6 %all-to-all-done.5 = f32[4,32,579]{2,1,0:T(8,128)} async-done(((f32[4,32,579]{2,1,0:T(8,128)}), f32[4,32,579]{2,1,0:T(8,128)}, u32[]{:S(2)}, u32[]{:S(2)}) %all-to-all-start.5) | async-done | bytes 296480 | tf_op jit(solution)/shard_map/all_to_all | solution.py:54
  157.2 1.2 copy.94
  159.5 0.8 reshape.295
  160.3 0.8 reshape.296
  (82 shorter events, 18.1 us)
Async XLA Ops:
  0.6 5.3 %copy-start = (bf16[1,2,2,69120]{3,2,1,0:T(2,128)(2,1)S(1)}, bf16[1,2,2,69120]{3,2,1,0:T(2,128)(2,1)}, u32[]{:S(2)}) copy-start(bf16[1,2,2,69120]{3,2,1,0:T(2,128)(2,1)} %param.8) | copy-start | bytes 1658884
  3.9 3.3 %copy-start.8 = (bf16[720,1,256]{2,0,1:T(8,128)(2,1)}, bf16[720,1,256]{2,0,1:T(8,128)(2,1)S(1)}, u32[]{:S(2)}) copy-start(bf16[720,1,256]{2,0,1:T(8,128)(2,1)S(1)} %get-tuple-element.18) | copy-start | bytes 1105924
  3.9 3.3 %copy-start.10 = (bf16[720,1,256]{2,0,1:T(8,128)(2,1)}, bf16[720,1,256]{2,0,1:T(8,128)(2,1)S(1)}, u32[]{:S(2)}) copy-start(bf16[720,1,256]{2,0,1:T(8,128)(2,1)S(1)} %get-tuple-element.19) | copy-start | bytes 1105924
  10.0 48.9 %all-to-all-start = ((bf16[2,2,2,256,2,96]{5,2,4,1,0,3:T(2,128)(2,1)}), bf16[2,2,2,256,2,96]{5,2,4,1,0,3:T(2,128)(2,1)S(1)}, u32[]{:S(2)}, u32[]{:S(2)}) async-start(bf16[2,2,2,256,2,96]{5,2,4,1,0,3:T(2,128)(2,1)} %copy.72), calls=%async_computation | async-start | bytes 2097152 | tf_op jit(solution)/shard_map/all_to_all | solution.py:21
  37.5 3.5 %copy-start.12 = (bf16[2,2,96]{2,1,0:T(2,128)(2,1)S(1)}, bf16[2,2,96]{2,1,0:T(2,128)(2,1)}, u32[]{:S(2)}) copy-start(bf16[2,2,96]{2,1,0:T(2,128)(2,1)} %param.10) | copy-start | bytes 2308
  59.1 1.4 copy-start.3
  59.1 1.4 copy-start.6
  59.9 1.1 copy-start.5
  61.4 1.1 copy-start.1
  65.8 1.0 copy-start.2
  66.0 1.1 copy-start.7
  69.0 17.1 %all-to-all-start.2 = ((f32[4,32,579]{2,1,0:T(8,128)}), f32[4,32,579]{2,1,0:T(8,128)S(1)}, u32[]{:S(2)}, u32[]{:S(2)}) async-start(f32[4,32,579]{2,1,0:T(8,128)} %copy.93), calls=%async_computation.2 | async-start | bytes 655360 | tf_op jit(solution)/shard_map/all_to_all | solution.py:35
  75.8 29.6 %copy-start.4 = (bf16[2,256,2,256]{3,2,1,0:T(2,128)(2,1)S(1)}, bf16[2,256,2,256]{3,2,1,0:T(2,128)(2,1)}, u32[]{:S(2)}) copy-start(bf16[2,256,2,256]{3,2,1,0:T(2,128)(2,1)} %convert_element_type.162) | copy-start | bytes 1572868
  86.8 14.0 %all-to-all-start.3 = ((f32[32,1,579]{2,1,0:T(1,128)}), f32[32,1,579]{2,1,0:T(1,128)S(1)}, u32[]{:S(2)}, u32[]{:S(2)}) async-start(f32[32,1,579]{2,1,0:T(1,128)} %all_to_all.45), calls=%async_computation.3 | async-start | bytes 163840 | tf_op jit(solution)/shard_map/all_to_all | solution.py:42
  101.6 13.9 %all-to-all-start.4 = ((f32[32,1,579]{2,1,0:T(1,128)}), f32[32,1,579]{2,1,0:T(1,128)S(1)}, u32[]{:S(2)}, u32[]{:S(2)}) async-start(f32[32,1,579]{2,1,0:T(1,128)} %broadcast_in_dim.6), calls=%async_computation.4 | async-start | bytes 163840 | tf_op jit(solution)/shard_map/all_to_all | solution.py:54
  115.5 26.4 %all-to-all-start.1 = ((bf16[1,2,2,2,256,96]{5,1,3,2,0,4:T(2,128)(2,1)}), bf16[1,2,2,2,256,96]{5,1,3,2,0,4:T(2,128)(2,1)S(1)}, u32[]{:S(2)}, u32[]{:S(2)}) async-start(bf16[1,2,2,2,256,96]{5,1,3,2,0,4:T(2,128)(2,1)} %copy.81), calls=%async_computation.1 | async-start | bytes 1048576 | tf_op jit(solution)/shard_map/all_to_all | solution.py:188
  142.6 4.9 %copy-start.9 = (bf16[720,1,256]{2,0,1:T(8,128)(2,1)S(1)}, bf16[720,1,256]{2,0,1:T(8,128)(2,1)}, u32[]{:S(2)}) copy-start(bf16[720,1,256]{2,0,1:T(8,128)(2,1)} %copy-done.8) | copy-start | bytes 1105924
  142.6 14.6 %all-to-all-start.5 = ((f32[4,32,579]{2,1,0:T(8,128)}), f32[4,32,579]{2,1,0:T(8,128)}, u32[]{:S(2)}, u32[]{:S(2)}) async-start(f32[4,32,579]{2,1,0:T(8,128)} %broadcast_in_dim.8), calls=%async_computation.5 | async-start | bytes 655360 | tf_op jit(solution)/shard_map/all_to_all | solution.py:54
  146.9 1.0 copy-start.11
where the time goes:
time: 162 us
  waiting for transfers between devices  69.9 us (43%)
  starting transfers between devices  46.2 us (29%)
  local copies, waits for them, and re-layouts  25.8 us (16%)
  other arithmetic  9.85 us (6%)
  matrix products  8.68 us (5%)
    all_to_all x1, starting transfers between devices, side_by_side(): lax.all_to_all(both, axis, split_axis=split_dim, concat_axis=concat_dim,...  19.6 us
    all_to_all x1, waiting for transfers between devices, local(): lax.all_to_all(returned, LAT, split_axis=4, concat_axis=3, tiled=True)  18.2 us
    all_to_all x1, waiting for transfers between devices, side_by_side(): lax.all_to_all(both, axis, split_axis=split_dim, concat_axis=concat_dim,...  17.7 us
    all_to_all x2, waiting for transfers between devices, sent_to_all(): lax.all_to_all(jnp.broadcast_to(shard[None], (devices, *shard.shape)), ax...  14.1 us
    all_to_all x1, waiting for transfers between devices, summed_on_arrival(): lax.all_to_all(parts, axis, split_axis=0, concat_axis=0, tiled=True)  10.2 us
    all_to_all x1, waiting for transfers between devices, sum_by_axis(): return jnp.sum(lax.all_to_all(own, far, 0, 0, tiled=True), axis=0)  9.68 us
    all_to_all x1, starting transfers between devices, local(): lax.all_to_all(returned, LAT, split_axis=4, concat_axis=3, tiled=True)  8.13 us
    all_to_all x2, starting transfers between devices, sent_to_all(): lax.all_to_all(jnp.broadcast_to(shard[None], (devices, *shard.shape)), ax...  8.1 us
  transfers between devices with their start and end apart: 6, of which 6 were waited for; matrix products, arithmetic and copies ran while one was open for 11% of the time, Pallas kernels for 0%

commit v1 on v0

v1 whole, which is shorter than its diff:
```python
import functools
import math

import jax
import jax.numpy as jnp
import ml_dtypes
import numpy as np
from jax import lax
from jax.experimental import pallas as pl
from jax.experimental.pallas import tpu as pltpu
from jax.sharding import Mesh
from jax.sharding import PartitionSpec as P

MESH = pl.DeviceIdType.MESH
NAMES = ("lat_0", "lat_1", "lat_2")
WIDTH = 96
LANES = 128
ROWS = 192
GROUPS = 180
F32 = jnp.float32
BF16 = jnp.bfloat16
FIRST = (0, 96, 64, 32)


def tables(devices):
    nlat, nlon = (2 * devices, 4 * GROUPS)
    w = np.arange(nlon)[:, None]
    k = np.arange(2 * devices)[None, :]
    phase = (w * k % nlon) * (2.0 * math.pi / nlon)
    east = np.stack([np.cos(phase), -np.sin(phase)], axis=1) / math.sqrt(nlon)
    east = east.reshape(GROUPS, 4, 2, devices, 2).transpose(1, 0, 2, 3, 4)
    filled = np.zeros((4, ROWS, 2, devices, 2))
    filled[:, :GROUPS] = east
    out_east = filled.transpose(4, 2, 3, 0, 1).reshape(2, 2 * devices, 4 * ROWS)
    back = np.zeros((2, 2, 4, ROWS, devices, 2, 2))
    for h in range(2):
        back[h, :, :, :, :, :, h] = filled.transpose(4, 0, 1, 3, 2)
    back = back.reshape(2, 2, 4 * ROWS, 4 * devices)
    q = np.arange(nlat)[:, None]
    h = np.arange(nlat)[None, :]
    phase = (q * h % nlat) * (2.0 * math.pi / nlat)
    cosine, sine = (np.cos(phase) / math.sqrt(nlat), np.sin(phase) / math.sqrt(nlat))
    north = np.stack([np.stack([cosine, sine]), np.stack([-sine, cosine])])
    north = north.transpose(0, 2, 1, 3).reshape(2, nlat // 4, 4, 2, devices, 2)
    north = north.transpose(0, 2, 1, 4, 3, 5).reshape(2 * nlat, devices, 4)
    both = np.zeros((2, 2 * nlat, devices, 2, 4))
    for f in range(2):
        both[f, :, :, f] = north
    both = both.reshape(4 * nlat, 8 * devices)
    turned = north.reshape(2 * nlat, 4 * devices).T
    return tuple(
        np.ascontiguousarray(t.astype(np.float32).astype(ml_dtypes.bfloat16))
        for t in (out_east, both, turned, back)
    )


def lane_of(shape):
    return lax.broadcasted_iota(jnp.int32, shape, 1)


def moved(block, start, end):
    shift = (end - start) % LANES
    return block if shift == 0 else pltpu.roll(block, shift, 1)


def block_of(tiles, i):
    if i == 0:
        return tiles[0]
    if i == 3:
        return tiles[2]
    lane = lane_of(tiles[0].shape)
    return jnp.where(lane >= FIRST[i], tiles[i - 1], tiles[i])


def tiles_of(blocks):
    lane = lane_of(blocks[0].shape)
    return [jnp.where(lane < FIRST[i + 1], blocks[i], blocks[i + 1]) for i in range(3)]


def dot(a, b):
    return lax.dot_general(a, b, (((1,), (0,)), ((), ())), preferred_element_type=F32)


def dot_rows(a, b):
    return lax.dot_general(a, b, (((0,), (0,)), ((), ())), preferred_element_type=F32)


def dot_turned(a, b):
    return lax.dot_general(a, b, (((1,), (1,)), ((), ())), preferred_element_type=F32)


def kernel(
    sizes,
    per_owner,
    owners,
    tok,
    cot,
    w_one,
    b_one,
    w_two,
    relu,
    shrink,
    east_t,
    north_t,
    turned_t,
    back_t,
    out,
    first_out,
    bias_out,
    second_out,
    raw,
    spread,
    packed,
    wide,
    ready,
    arrived,
    stacked,
    masks,
    relu_f,
    shrink_f,
    weights,
    square,
    bias_row,
    modes,
    upstream,
    hidden,
    inner,
    grad_modes,
    leaving,
    returned,
    back_rows,
    own_sums,
    all_sums,
    shared,
    result,
    result_out,
    east_v,
    north_v,
    turned_v,
    back_v,
    w_one_v,
    b_one_v,
    w_two_v,
    load_sem,
    self_sem,
    send_sem,
    recv_sem,
    plane_sem,
):
    nx, nz, ny = sizes
    devices = nx * nz * ny
    nlat = 2 * devices
    quarter = nlat // 4
    cx, cz, cy = (lax.axis_index(n) for n in NAMES)
    me = (cx * nz + cz) * ny + cy

    def whom(x, z, y):
        return dict(zip(NAMES, (x, z, y)))

    def at_index(p):
        return whom(p // (nz * ny), lax.rem(p // ny, nz), lax.rem(p, ny))

    barrier = pltpu.get_barrier_semaphore()
    line = [whom(cx, lax.rem(cz + i, nz), cy) for i in range(1, nz)]
    plane = [
        whom(lax.rem(cx + i, nx), cz, lax.rem(cy + j, ny))
        for i in range(nx)
        for j in range(ny)
        if i or j
    ]
    for d in line + plane:
        pl.semaphore_signal(barrier, inc=1, device_id=d, device_id_type=MESH)

    loads = [
        pltpu.make_async_copy(src, dst, load_sem.at[i])
        for i, (src, dst) in enumerate(
            (
                (tok, raw.at[0]),
                (cot, raw.at[1]),
                (east_t, east_v),
                (relu, masks.at[0]),
                (shrink, masks.at[1]),
                (w_one, w_one_v),
                (b_one, b_one_v),
                (w_two, w_two_v),
                (north_t, north_v),
                (turned_t, turned_v),
                (back_t, back_v),
            )
        )
    ]
    for c in loads:
        c.start()

    lane = lane_of((ROWS, LANES))
    for i in range(4):
        spread[i, pl.ds(6 * GROUPS, 6 * (ROWS - GROUPS)), :] = jnp.zeros(
            (6 * (ROWS - GROUPS), LANES), F32
        )
    for f in range(2):
        loads[f].wait()
        for h in range(2):
            i = 2 * f + h
            spread[i, pl.ds(0, 6 * GROUPS), :] = raw[f, h].astype(F32)
            for j in range(4):
                b = [
                    block_of(
                        [spread[i, pl.ds(2 * c + n, ROWS, stride=6), :] for c in range(3)], j
                    )
                    for n in range(2)
                ]
                a0 = moved(b[0], FIRST[j], FIRST[0])
                a1 = moved(b[1], FIRST[j], FIRST[1])
                a2 = moved(b[0], FIRST[j], FIRST[2])
                a3 = moved(b[1], FIRST[j], FIRST[3])
                zero = jnp.zeros_like(a0)
                four = (
                    jnp.where(lane < 96, a0, a1),
                    jnp.where(lane < 64, a1, zero),
                    jnp.where(lane < 64, zero, a2),
                    jnp.where(lane < 32, a2, a3),
                )
                for t, v in enumerate(four):
                    packed[i, pl.ds(j * ROWS, ROWS), pl.ds(t * LANES, LANES)] = v.astype(BF16)
            if i == 0:
                loads[2].wait()
            for s in range(2):
                rows = pl.ds(s * devices, devices)
                even = dot(east_v[0, rows, :], packed[i, :, pl.ds(0, 256)])
                odd = dot(east_v[1, rows, :], packed[i, :, pl.ds(256, 256)])
                to = pl.ds(4 * f + 2 * s + h, devices, stride=8)
                wide[0, to, :] = even[:, :128]
                wide[1, to, :] = even[:, 128:] + odd[:, :128]
                wide[2, to, :] = odd[:, 128:]
        if f == 0:
            pl.semaphore_wait(barrier, len(line) + len(plane))
            for d in plane:
                pl.semaphore_signal(plane_sem, inc=1, device_id=d, device_id_type=MESH)
    for c in range(3):
        ready[:, :, pl.ds(c * LANES, LANES)] = wide[c].reshape(devices, 8, LANES).astype(BF16)
    pl.semaphore_wait(plane_sem, len(plane))

    def exchange(src, dst, n):
        def send(i, carry):
            p = lax.rem(me + i, devices)
            pltpu.make_async_remote_copy(
                src.at[pl.ds(p, 1)],
                dst.at[pl.ds(me, 1)],
                send_sem.at[n],
                recv_sem.at[n],
                device_id=at_index(p),
                device_id_type=MESH,
            ).start()
            return carry

        lax.fori_loop(1, devices, send, 0)
        own = pltpu.make_async_copy(src.at[pl.ds(me, 1)], dst.at[pl.ds(me, 1)], self_sem.at[n])
        own.start()
        many = pl.ds(0, devices - 1)
        whole = pltpu.make_async_remote_copy(
            src.at[many],
            dst.at[many],
            send_sem.at[n],
            recv_sem.at[n],
            device_id=whom(cx, lax.rem(cz + 1, nz), cy),
            device_id_type=MESH,
        )
        return own, whole

    own, whole = exchange(ready, arrived, 0)

    for c in loads[3:8]:
        c.wait()
    for m, to in ((0, relu_f), (1, shrink_f)):
        for s in range(2):
            for j in range(4):
                blocks = []
                for kn in range(4):
                    k, n = divmod(kn, 2)
                    three = [
                        masks[m, 2 * s + n, pl.ds(2 * c + k, quarter, stride=6), :]
                        for c in range(3)
                    ]
                    blocks.append(moved(block_of(three, j), FIRST[j], FIRST[kn]))
                for c, v in enumerate(tiles_of(blocks)):
                    to[pl.ds(s * nlat + j * quarter, quarter), pl.ds(c * LANES, LANES)] = v.astype(
                        F32
                    )
    square[...] = jnp.zeros_like(square)
    weights[...] = jnp.zeros_like(weights)
    column = lane_of((WIDTH, LANES))
    for m, src in ((0, w_one_v), (1, w_two_v)):
        for t in range(2):
            for n in range(2):
                square[:, pl.ds(0, WIDTH)] = src[t, n].astype(F32)
                base = square[...]
                for k in range(2):
                    kn = 2 * k + n
                    turned = moved(base, 0, FIRST[kn])
                    rows = pl.ds(kn * WIDTH, WIDTH)
                    if kn < 3:
                        keep = column >= FIRST[kn] if kn else column < WIDTH
                        c = (0, 0, 1)[kn]
                        weights[2 * m + t, rows, pl.ds(c * LANES, LANES)] = jnp.where(
                            keep, turned, 0.0
                        ).astype(BF16)
                    if kn > 0:
                        keep = column >= FIRST[3] if kn == 3 else column < FIRST[kn + 1]
                        c = (0, 1, 2, 2)[kn]
                        weights[2 * m + t, rows, pl.ds(c * LANES, LANES)] = jnp.where(
                            keep, turned, 0.0
                        ).astype(BF16)
    for t in range(2):
        for n in range(2):
            bias_row[pl.ds(2 * t + n, 1), pl.ds(0, WIDTH)] = b_one_v[t, pl.ds(n, 1), :].astype(F32)
    for t in range(2):
        blocks = [
            moved(
                jnp.broadcast_to(bias_row[pl.ds(2 * t + kn % 2, 1), pl.ds(0, LANES)], (8, LANES)),
                0,
                FIRST[kn],
            )
            for kn in range(4)
        ]
        for c, v in enumerate(tiles_of(blocks)):
            bias_row[pl.ds(8 + 8 * t, 8), pl.ds(c * LANES, LANES)] = v

    for c in loads[8:10]:
        c.wait()
    own.wait()
    whole.wait_recv()
    stacked[...] = arrived[...].reshape(8 * devices, 384)
    chunk = min(256, nlat)
    for f in (1, 0):
        for a in range(0, 2 * nlat, chunk):
            rows = pl.ds(a, chunk)
            value = dot(north_v[pl.ds(2 * f * nlat + a, chunk), :], stacked[...]).astype(BF16)
            if f:
                upstream[rows, :] = (value.astype(F32) * shrink_f[rows, :]).astype(BF16)
            else:
                modes[rows, :] = value

    half = min(128, nlat)
    parts = [(pl.ds(a, half), pl.ds(nlat + a, half)) for a in range(0, nlat, half)]

    def conjugate_mix(src, top, low, m):
        a, b = (src[top, :], src[low, :])
        real = dot_turned(a, weights[2 * m]) + dot_turned(b, weights[2 * m + 1])
        imag = dot_turned(b, weights[2 * m]) - dot_turned(a, weights[2 * m + 1])
        return real, imag

    for top, low in parts:
        real, imag = conjugate_mix(upstream, top, low, 1)
        inner[top, :] = (relu_f[top, :] * real).astype(BF16)
        inner[low, :] = (relu_f[low, :] * imag).astype(BF16)
    for top, low in parts:
        real, imag = conjugate_mix(inner, top, low, 0)
        grad_modes[top, :] = real.astype(BF16)
        grad_modes[low, :] = imag.astype(BF16)
    for a in range(0, 4 * devices, half):
        value = dot(turned_v[pl.ds(a, half), :], grad_modes[...]).astype(BF16)
        leaving[pl.ds(a // 4, half // 4)] = value.reshape(half // 4, 4, 384)

    own_back, whole_back = exchange(leaving, returned, 1)

    for top, low in parts:
        a, b = (modes[top, :], modes[low, :])
        real = dot(a, weights[0]) - dot(b, weights[1]) + bias_row[pl.ds(8, 1), :]
        imag = dot(a, weights[1]) + dot(b, weights[0]) + bias_row[pl.ds(16, 1), :]
        hidden[top, :] = (relu_f[top, :] * real).astype(BF16)
        hidden[low, :] = (relu_f[low, :] * imag).astype(BF16)
    upper, lower = (pl.ds(0, nlat), pl.ds(nlat, nlat))

    def diagonal(product, n):
        total = None
        for k in range(2):
            kn = 2 * k + n
            rows = product[kn * WIDTH : (kn + 1) * WIDTH]
            tiles = [rows[:, c * LANES : (c + 1) * LANES] for c in range(3)]
            block = moved(block_of(tiles, kn), FIRST[kn], 0)
            total = block if total is None else total + block
        return jnp.where(column < WIDTH, total, 0.0)

    eighth = WIDTH // 8
    for g, (left, right) in enumerate(((modes, inner), (hidden, upstream))):
        real = dot_rows(left[...], right[...])
        imag = dot_rows(left[upper, :], right[lower, :]) - dot_rows(left[lower, :], right[upper, :])
        for t, product in enumerate((real, imag)):
            for n in range(2):
                m = 4 * g + 2 * t + n
                shared[pl.ds(m * eighth, eighth)] = (
                    diagonal(product, n).reshape(eighth, 8, LANES).astype(BF16)
                )
    row8 = lax.broadcasted_iota(jnp.int32, (8, LANES), 0)
    total = jnp.zeros((8, LANES), F32)
    for t in range(2):
        sums = jnp.sum(inner[pl.ds(t * nlat, nlat), :].astype(F32), axis=0, keepdims=True)
        tiles = [
            jnp.broadcast_to(sums[:, c * LANES : (c + 1) * LANES], (8, LANES)) for c in range(3)
        ]
        for n in range(2):
            value = moved(block_of(tiles, n), FIRST[n], 0) + moved(
                block_of(tiles, 2 + n), FIRST[2 + n], 0
            )
            total = jnp.where(row8 == 2 * t + n, value, total)
    shared[8 * eighth] = total.astype(BF16)

    def to_owner(i, carry):
        p = lax.rem(me + i, devices)

        @pl.when(p < owners)
        def _():
            pltpu.make_async_remote_copy(
                shared.at[pl.ds(p * per_owner, per_owner)],
                own_sums.at[me],
                send_sem.at[2],
                recv_sem.at[2],
                device_id=at_index(p),
                device_id_type=MESH,
            ).start()

        return carry

    lax.fori_loop(1, devices, to_owner, 0)
    whole.wait_send()

    neighbour = whom(cx, lax.rem(cz + 1, nz), cy)

    def bytes_of(ref, n):
        return pltpu.make_async_remote_copy(
            ref,
            ref,
            send_sem.at[n],
            recv_sem.at[n],
            device_id=neighbour,
            device_id_type=MESH,
        )

    @pl.when(me < owners)
    def _():
        own_sums[me] = shared[pl.ds(me * per_owner, per_owner)]
        bytes_of(own_sums.at[pl.ds(0, devices - 1)], 2).wait_recv()
        all_sums[me] = jnp.sum(own_sums[...].astype(F32), axis=0).astype(BF16)

        def to_all(i, carry):
            pltpu.make_async_remote_copy(
                all_sums.at[me],
                all_sums.at[me],
                send_sem.at[3],
                recv_sem.at[3],
                device_id=at_index(lax.rem(me + i, devices)),
                device_id_type=MESH,
            ).start()
            return carry

        lax.fori_loop(1, devices, to_all, 0)

    loads[10].wait()
    own_back.wait()
    whole_back.wait_recv()
    back_rows[...] = returned[...].reshape(4 * devices, 384)
    for h in range(2):
        for j in range(4):
            rows = pl.ds(j * ROWS, ROWS)
            even = dot(back_v[h, 0, rows, :], back_rows[:, pl.ds(0, 256)])
            odd = dot(back_v[h, 1, rows, :], back_rows[:, pl.ds(128, 256)])
            tiles = (even[:, :128], even[:, 128:], None)
            parted = (None, odd[:, :128], odd[:, 128:])
            for n in range(2):
                value = moved(block_of(tiles, n), FIRST[n], FIRST[j]) + moved(
                    block_of(parted, 2 + n), FIRST[2 + n], FIRST[j]
                ) if n == 1 else moved(tiles[0], FIRST[0], FIRST[j]) + moved(
                    jnp.where(lane >= FIRST[2], parted[1], parted[2]), FIRST[2], FIRST[j]
                )
                result_out[j, n] = value
        for n in range(2):
            for c, v in enumerate(tiles_of([result_out[j, n] for j in range(4)])):
                result[h, pl.ds(2 * c + n, ROWS, stride=6), :] = v
        done = result[h, pl.ds(0, 6 * GROUPS), :] + raw[1, h].astype(F32)
        raw[0, h] = done.astype(BF16)
    store = pltpu.make_async_copy(raw.at[0], out, load_sem.at[0])
    store.start()

    whole_back.wait_send()

    @pl.when(me < owners)
    def _():
        bytes_of(shared.at[pl.ds(0, (owners - 1) * per_owner)], 2).wait_send()
        bytes_of(own_sums.at[pl.ds(0, devices - 1)], 3).wait_send()
        bytes_of(all_sums.at[pl.ds(0, owners - 1)], 3).wait_recv()

    @pl.when(me >= owners)
    def _():
        bytes_of(shared.at[pl.ds(0, owners * per_owner)], 2).wait_send()
        bytes_of(all_sums.at[pl.ds(0, owners)], 3).wait_recv()

    factor = 1.0 / math.sqrt(nlat * 2 * devices)
    sums = all_sums[...].reshape(owners * per_owner * 8, LANES)
    for g, ref in enumerate((first_out, second_out)):
        for t in range(2):
            for n in range(2):
                m = 4 * g + 2 * t + n
                ref[t, n] = sums[m * WIDTH : (m + 1) * WIDTH, :WIDTH].astype(F32) * factor
    last = sums[8 * WIDTH : 8 * WIDTH + 8].astype(F32) * factor
    for t in range(2):
        bias_out[t] = last[2 * t : 2 * t + 2, :WIDTH]
    store.wait()


def local(sizes, tokens, cotangent, first_weight, first_bias, second_weight, relu_mask, shrink_mask):
    devices = math.prod(sizes)
    nlat = 2 * devices
    blocks = 8 * WIDTH // 8 + 1
    per_owner = -(-blocks // devices)
    owners = -(-blocks // per_owner)

    def in_rows(field):
        return (
            field.reshape(2, 2, 3 * GROUPS, LANES)
            .transpose(0, 2, 1, 3)
            .reshape(2, 6 * GROUPS, LANES)
        )

    def mask_rows(mask):
        width = mask.shape[-1] // LANES
        return (
            mask.reshape(4, 2, width, LANES).transpose(0, 2, 1, 3).reshape(4, 2 * width, LANES)
        )

    constants = [jnp.asarray(t) for t in tables(devices)]
    anywhere = pl.BlockSpec(memory_space=pl.ANY)
    in_vmem = pl.BlockSpec(memory_space=pltpu.VMEM)

    def vmem(*shape, dtype=BF16):
        return pltpu.VMEM(shape, dtype)

    out, first, bias, second = pl.pallas_call(
        functools.partial(kernel, sizes, per_owner, owners),
        out_shape=(
            jax.ShapeDtypeStruct((2, 6 * GROUPS, LANES), BF16),
            jax.ShapeDtypeStruct(first_weight.shape, F32),
            jax.ShapeDtypeStruct(first_bias.shape, F32),
            jax.ShapeDtypeStruct(second_weight.shape, F32),
        ),
        in_specs=[anywhere] * 11,
        out_specs=(anywhere, in_vmem, in_vmem, in_vmem),
        scratch_shapes=[
            vmem(2, 2, 6 * GROUPS, LANES),
            vmem(4, 6 * ROWS, LANES, dtype=F32),
            vmem(4, 4 * ROWS, 4 * LANES),
            vmem(3, 8 * devices, LANES, dtype=F32),
            vmem(devices, 8, 384),
            vmem(devices, 8, 384),
            vmem(8 * devices, 384),
            vmem(2, 4, 6 * (nlat // 4), LANES, dtype=jnp.int32),
            vmem(2 * nlat, 384, dtype=F32),
            vmem(2 * nlat, 384, dtype=F32),
            vmem(4, 384, 384),
            vmem(WIDTH, LANES, dtype=F32),
            vmem(24, 384, dtype=F32),
            vmem(2 * nlat, 384),
            vmem(2 * nlat, 384),
            vmem(2 * nlat, 384),
            vmem(2 * nlat, 384),
            vmem(2 * nlat, 384),
            vmem(devices, 4, 384),
            vmem(devices, 4, 384),
            vmem(4 * devices, 384),
            vmem(devices, per_owner, 8, LANES),
            vmem(owners, per_owner, 8, LANES),
            vmem(owners * per_owner, 8, LANES),
            vmem(2, 6 * ROWS, LANES, dtype=F32),
            vmem(4, 2, ROWS, LANES, dtype=F32),
            vmem(*constants[0].shape),
            vmem(*constants[1].shape),
            vmem(*constants[2].shape),
            vmem(*constants[3].shape),
            vmem(*first_weight.shape),
            vmem(*first_bias.shape),
            vmem(*second_weight.shape),
            pltpu.SemaphoreType.DMA((11,)),
            pltpu.SemaphoreType.DMA((2,)),
            pltpu.SemaphoreType.DMA((4,)),
            pltpu.SemaphoreType.DMA((4,)),
            pltpu.SemaphoreType.REGULAR,
        ],
        compiler_params=pltpu.CompilerParams(
            collective_id=0, has_side_effects=True, vmem_limit_bytes=48 * 1024 * 1024
        ),
    )(
        in_rows(tokens),
        in_rows(cotangent),
        first_weight,
        first_bias,
        second_weight,
        mask_rows(relu_mask),
        mask_rows(shrink_mask),
        *constants,
    )
    token_gradient = (
        out.reshape(2, 3 * GROUPS, 2, LANES).transpose(0, 2, 1, 3).reshape(tokens.shape)
    )
    return (token_gradient, first, bias, second)


def solution(mesh, sizes=(4, 8, 4)):
    finer = Mesh(mesh.devices.reshape(*sizes, mesh.shape["ch"]), (*NAMES, "ch"))
    in_specs = (
        P(None, NAMES, "ch", None),
        P(None, NAMES, "ch", None),
        P(None, "ch", None, None),
        P(None, "ch", None),
        P(None, "ch", None, None),
        P(None, None, "ch", NAMES, None),
        P(None, None, "ch", NAMES, None),
    )
    out_specs = (
        P(None, NAMES, "ch", None),
        P(None, "ch", None, None),
        P(None, "ch", None),
        P(None, "ch", None, None),
    )
    return jax.shard_map(
        functools.partial(local, sizes),
        mesh=finer,
        in_specs=in_specs,
        out_specs=out_specs,
        check_vma=False,
    )
```

time: 162 us -> 85.6 us (0.53)
  the two profiles are of different devices: /device:TPU:8 before, /device:TPU:64 now
where the time goes in v1:
time: 85.6 us; the launch traced here: 85.2 us
  Pallas kernels  70.8 us (83%)
  local copies, waits for them, and re-layouts  13.6 us (16%)
    pallas_call x1, Pallas kernels, local(): pl.pallas_call(functools.partial(kernel, sizes, per_owner, owners), out_s...  70.8 us
    unnamed x21, local copies, waits for them, and re-layouts  5.37 us
    reshape x2, local copies, waits for them, and re-layouts, in_rows(): field.reshape(2, 2, 3 * GROUPS, LANES).transpose(0, 2, 1, 3)  4.34 us
    transpose x2, local copies, waits for them, and re-layouts, in_rows(): return field.reshape(2, 2, 3 * GROUPS, LANES).transpose(0, 2, 1, 3).resha...  2.96 us

profile of v1, /device:TPU:64, one launch (start us, length us, event | category | flops | bytes accessed | tf_op | source)
XLA Modules:
  0.0 85.2 jit_solution(16233042200237814646)
XLA Ops:
  0.6 0.0 copy-start.3
  0.6 0.0 copy-start.2
  0.7 0.0 copy-start.1
  0.7 0.0 copy-start
  0.7 0.0 copy-start.8
  0.7 0.0 copy-start.6
  0.7 2.2 %reshape.38 = bf16[2,2,540,128]{3,2,1,0:T(8,128)(2,1)} reshape(bf16[1,2,2,69120]{3,2,1,0:T(2,128)(2,1)} %param.11) | data formatting | bytes 1105920 | tf_op jit(solution)/shard_map/reshape | solution.py:519
  2.9 1.5 %copy.20 = bf16[2,540,2,128]{3,2,1,0:T(2,128)(2,1)S(1)} copy(bf16[2,540,2,128]{3,1,2,0:T(8,128)(2,1)} %bitcast.24) | data formatting | bytes 1105920 | tf_op jit(solution)/shard_map/transpose | solution.py:520
  4.4 2.1 %reshape.40 = bf16[2,2,540,128]{3,2,1,0:T(8,128)(2,1)} reshape(bf16[1,2,2,69120]{3,2,1,0:T(2,128)(2,1)} %param.12) | data formatting | bytes 1105920 | tf_op jit(solution)/shard_map/reshape | solution.py:519
  6.5 1.5 %copy.21 = bf16[2,540,2,128]{3,2,1,0:T(2,128)(2,1)S(1)} copy(bf16[2,540,2,128]{3,1,2,0:T(8,128)(2,1)} %bitcast.25) | data formatting | bytes 1105920 | tf_op jit(solution)/shard_map/transpose | solution.py:520
  8.0 0.0 copy-done.3
  8.0 0.0 copy-done.2
  8.0 0.0 copy-done.1
  8.0 0.0 copy-done
  8.0 0.0 copy-done.8
  8.1 0.0 copy-done.6
  8.1 0.0 copy-start.7
  8.1 0.9 %copy-done.7 = bf16[2,2,96,96]{3,2,1,0:T(8,128)(2,1)S(1)} copy-done((bf16[2,2,96,96]{3,2,1,0:T(8,128)(2,1)S(1)}, bf16[2,2,96,96]{3,2,1,0:T(8,128)(2,1)}, u32[]{:S(2)}) %copy-start.7) | copy-done | bytes 73752
  9.0 70.8 %shard_map.138 = (bf16[2,1080,128]{2,1,0:T(8,128)(2,1)S(1)}, f32[2,2,96,96]{3,2,1,0:T(8,128)S(1)}, f32[2,2,96]{2,1,0:T(2,128)S(1)}, f32[2,2,96,96]{3,2,1,0:T(8,128)S(1)}) custom-call(bf16[2,1080,128]{2,1,0:T(8,128)(2,1)S(1)} %bitcast.18, bf16[2,1080,128]{2,1,0:T(8,128)(2,1)S(1)} %bitcast.19, bf16[2,2,96,96]{3,2,1,0:T(8,128)(2,1)S(1)} %copy-done.6, ...), custom_call_target="tpu_custom_call" | custom-call | tf_op jit(solution)/shard_map/pallas_call | solution.py:537
  79.8 0.0 copy-start.4
  79.8 0.0 copy-start.5
  79.8 0.1 copy.26
  79.9 0.6 copy-done.4
  80.5 0.1 copy-done.5
  80.5 0.9 %reshape.47 = bf16[1,2,2,69120]{3,2,1,0:T(2,128)(2,1)} reshape(bf16[2,2,540,128]{3,2,1,0:T(8,128)(2,1)S(1)} %bitcast.23) | data formatting | bytes 1105920 | tf_op jit(solution)/shard_map/reshape | solution.py:601
  81.4 1.6 %copy.30 = f32[2,2,96,96]{3,2,1,0:T(8,128)} copy(f32[2,2,96,96]{3,2,1,0:T(8,128)} %copy-done.5) | data formatting | bytes 294912
  83.0 0.6 copy.31
  83.6 1.6 %copy.32 = f32[2,2,96,96]{3,2,1,0:T(8,128)} copy(f32[2,2,96,96]{3,2,1,0:T(8,128)} %copy-done.4) | data formatting | bytes 294912
Async XLA Ops:
  0.6 7.4 %copy-start.3 = (bf16[512,512]{1,0:T(8,128)(2,1)S(1)}, bf16[512,512]{1,0:T(8,128)(2,1)}, u32[]{:S(2)}) copy-start(bf16[512,512]{1,0:T(8,128)(2,1)} %constant.10.clone.turned_t) | copy-start | bytes 1572868
  0.6 7.4 %copy-start.2 = (bf16[2,256,768]{2,1,0:T(8,128)(2,1)S(1)}, bf16[2,256,768]{2,1,0:T(8,128)(2,1)}, u32[]{:S(2)}) copy-start(bf16[2,256,768]{2,1,0:T(8,128)(2,1)} %constant.8.clone.east_t) | copy-start | bytes 2359300
  0.7 7.4 %copy-start.1 = (s32[1,2,2,2,24576]{4,3,2,1,0:T(2,128)S(1)}, s32[1,2,2,2,24576]{4,3,2,1,0:T(2,128)}, u32[]{:S(2)}) copy-start(s32[1,2,2,2,24576]{4,3,2,1,0:T(2,128)} %param.17) | copy-start | bytes 2359300
  0.7 7.4 %copy-start = (s32[1,2,2,2,24576]{4,3,2,1,0:T(2,128)S(1)}, s32[1,2,2,2,24576]{4,3,2,1,0:T(2,128)}, u32[]{:S(2)}) copy-start(s32[1,2,2,2,24576]{4,3,2,1,0:T(2,128)} %param.16) | copy-start | bytes 2359300
  0.7 7.4 %copy-start.8 = (bf16[2,2,96]{2,1,0:T(2,128)(2,1)S(1)}, bf16[2,2,96]{2,1,0:T(2,128)(2,1)}, u32[]{:S(2)}) copy-start(bf16[2,2,96]{2,1,0:T(2,128)(2,1)} %b_one.1) | copy-start | bytes 2308
  0.7 7.4 %copy-start.6 = (bf16[2,2,96,96]{3,2,1,0:T(8,128)(2,1)S(1)}, bf16[2,2,96,96]{3,2,1,0:T(8,128)(2,1)}, u32[]{:S(2)}) copy-start(bf16[2,2,96,96]{3,2,1,0:T(8,128)(2,1)} %w_one.1) | copy-start | bytes 221188
  8.1 0.9 %copy-start.7 = (bf16[2,2,96,96]{3,2,1,0:T(8,128)(2,1)S(1)}, bf16[2,2,96,96]{3,2,1,0:T(8,128)(2,1)}, u32[]{:S(2)}) copy-start(bf16[2,2,96,96]{3,2,1,0:T(8,128)(2,1)} %w_two.1) | copy-start | bytes 221188
  79.8 0.7 copy-start.4
  79.8 0.7 copy-start.5

commit v2 on v1

--- a/solution.py
+++ b/solution.py
@@ -7,6 +7,7 @@
 import numpy as np
 from jax import lax
 from jax.experimental import pallas as pl
+from jax.experimental.layout import Layout, with_layout_constraint
 from jax.experimental.pallas import tpu as pltpu
 from jax.sharding import Mesh
 from jax.sharding import PartitionSpec as P
@@ -105,9 +106,7 @@
     turned_t,
     back_t,
     out,
-    first_out,
-    bias_out,
-    second_out,
+    all_sums,
     raw,
     spread,
     packed,
@@ -130,7 +129,6 @@
     returned,
     back_rows,
     own_sums,
-    all_sums,
     shared,
     result,
     result_out,
@@ -145,7 +143,6 @@
     self_sem,
     send_sem,
     recv_sem,
-    plane_sem,
 ):
     nx, nz, ny = sizes
     devices = nx * nz * ny
@@ -161,15 +158,11 @@
         return whom(p // (nz * ny), lax.rem(p // ny, nz), lax.rem(p, ny))
 
     barrier = pltpu.get_barrier_semaphore()
-    line = [whom(cx, lax.rem(cz + i, nz), cy) for i in range(1, nz)]
-    plane = [
-        whom(lax.rem(cx + i, nx), cz, lax.rem(cy + j, ny))
-        for i in range(nx)
-        for j in range(ny)
-        if i or j
-    ]
-    for d in line + plane:
+
+    def greet(i, carry):
+        d = at_index(lax.rem(me + i, devices))
         pl.semaphore_signal(barrier, inc=1, device_id=d, device_id_type=MESH)
+        return carry
 
     loads = [
         pltpu.make_async_copy(src, dst, load_sem.at[i])
@@ -191,6 +184,7 @@
     ]
     for c in loads:
         c.start()
+    lax.fori_loop(1, devices, greet, 0)
 
     lane = lane_of((ROWS, LANES))
     for i in range(4):
@@ -232,13 +226,9 @@
                 wide[0, to, :] = even[:, :128]
                 wide[1, to, :] = even[:, 128:] + odd[:, :128]
                 wide[2, to, :] = odd[:, 128:]
-        if f == 0:
-            pl.semaphore_wait(barrier, len(line) + len(plane))
-            for d in plane:
-                pl.semaphore_signal(plane_sem, inc=1, device_id=d, device_id_type=MESH)
     for c in range(3):
         ready[:, :, pl.ds(c * LANES, LANES)] = wide[c].reshape(devices, 8, LANES).astype(BF16)
-    pl.semaphore_wait(plane_sem, len(plane))
+    pl.semaphore_wait(barrier, devices - 1)
 
     def exchange(src, dst, n):
         def send(i, carry):
@@ -354,16 +344,6 @@
         inner[top, :] = (relu_f[top, :] * real).astype(BF16)
         inner[low, :] = (relu_f[low, :] * imag).astype(BF16)
     for top, low in parts:
-        real, imag = conjugate_mix(inner, top, low, 0)
-        grad_modes[top, :] = real.astype(BF16)
-        grad_modes[low, :] = imag.astype(BF16)
-    for a in range(0, 4 * devices, half):
-        value = dot(turned_v[pl.ds(a, half), :], grad_modes[...]).astype(BF16)
-        leaving[pl.ds(a // 4, half // 4)] = value.reshape(half // 4, 4, 384)
-
-    own_back, whole_back = exchange(leaving, returned, 1)
-
-    for top, low in parts:
         a, b = (modes[top, :], modes[low, :])
         real = dot(a, weights[0]) - dot(b, weights[1]) + bias_row[pl.ds(8, 1), :]
         imag = dot(a, weights[1]) + dot(b, weights[0]) + bias_row[pl.ds(16, 1), :]
@@ -371,26 +351,27 @@
         hidden[low, :] = (relu_f[low, :] * imag).astype(BF16)
     upper, lower = (pl.ds(0, nlat), pl.ds(nlat, nlat))
 
-    def diagonal(product, n):
+    def diagonal(product, n, start):
         total = None
         for k in range(2):
             kn = 2 * k + n
             rows = product[kn * WIDTH : (kn + 1) * WIDTH]
             tiles = [rows[:, c * LANES : (c + 1) * LANES] for c in range(3)]
-            block = moved(block_of(tiles, kn), FIRST[kn], 0)
+            block = moved(block_of(tiles, kn), FIRST[kn], start)
             total = block if total is None else total + block
-        return jnp.where(column < WIDTH, total, 0.0)
+        return total
 
     eighth = WIDTH // 8
     for g, (left, right) in enumerate(((modes, inner), (hidden, upstream))):
         real = dot_rows(left[...], right[...])
         imag = dot_rows(left[upper, :], right[lower, :]) - dot_rows(left[lower, :], right[upper, :])
-        for t, product in enumerate((real, imag)):
-            for n in range(2):
-                m = 4 * g + 2 * t + n
-                shared[pl.ds(m * eighth, eighth)] = (
-                    diagonal(product, n).reshape(eighth, 8, LANES).astype(BF16)
-                )
+        blocks = [
+            diagonal(product, n, FIRST[2 * t + n])
+            for t, product in enumerate((real, imag))
+            for n in range(2)
+        ]
+        for c, v in enumerate(tiles_of(blocks)):
+            shared[pl.ds((3 * g + c) * eighth, eighth)] = v.reshape(eighth, 8, LANES).astype(BF16)
     row8 = lax.broadcasted_iota(jnp.int32, (8, LANES), 0)
     total = jnp.zeros((8, LANES), F32)
     for t in range(2):
@@ -403,12 +384,12 @@
                 block_of(tiles, 2 + n), FIRST[2 + n], 0
             )
             total = jnp.where(row8 == 2 * t + n, value, total)
-    shared[8 * eighth] = total.astype(BF16)
+    shared[6 * eighth] = total.astype(BF16)
 
     def to_owner(i, carry):
-        p = lax.rem(me + i, devices)
-
-        @pl.when(p < owners)
+        p = lax.rem(me + i, owners)
+
+        @pl.when(p != me)
         def _():
             pltpu.make_async_remote_copy(
                 shared.at[pl.ds(p * per_owner, per_owner)],
@@ -421,8 +402,18 @@
 
         return carry
 
-    lax.fori_loop(1, devices, to_owner, 0)
+    lax.fori_loop(0, owners, to_owner, 0)
     whole.wait_send()
+
+    for top, low in parts:
+        real, imag = conjugate_mix(inner, top, low, 0)
+        grad_modes[top, :] = real.astype(BF16)
+        grad_modes[low, :] = imag.astype(BF16)
+    for a in range(0, 4 * devices, half):
+        value = dot(turned_v[pl.ds(a, half), :], grad_modes[...]).astype(BF16)
+        leaving[pl.ds(a // 4, half // 4)] = value.reshape(half // 4, 4, 384)
+
+    own_back, whole_back = exchange(leaving, returned, 1)
 
     neighbour = whom(cx, lax.rem(cz + 1, nz), cy)
 
@@ -477,9 +468,7 @@
             for c, v in enumerate(tiles_of([result_out[j, n] for j in range(4)])):
                 result[h, pl.ds(2 * c + n, ROWS, stride=6), :] = v
         done = result[h, pl.ds(0, 6 * GROUPS), :] + raw[1, h].astype(F32)
-        raw[0, h] = done.astype(BF16)
-    store = pltpu.make_async_copy(raw.at[0], out, load_sem.at[0])
-    store.start()
+        out[h] = done.astype(BF16)
 
     whole_back.wait_send()
 
@@ -494,14 +483,22 @@
         bytes_of(shared.at[pl.ds(0, owners * per_owner)], 2).wait_send()
         bytes_of(all_sums.at[pl.ds(0, owners)], 3).wait_recv()
 
-    factor = 1.0 / math.sqrt(nlat * 2 * devices)
-    sums = all_sums[...].reshape(owners * per_owner * 8, LANES)
+
+def finish(factor, ahead, sums, out, first_out, bias_out, second_out, sem):
+    store = pltpu.make_async_copy(ahead, out, sem)
+    store.start()
+    eighth = WIDTH // 8
     for g, ref in enumerate((first_out, second_out)):
+        tiles = [
+            sums[pl.ds((3 * g + c) * eighth, eighth)].reshape(WIDTH, LANES).astype(F32)
+            for c in range(3)
+        ]
         for t in range(2):
             for n in range(2):
-                m = 4 * g + 2 * t + n
-                ref[t, n] = sums[m * WIDTH : (m + 1) * WIDTH, :WIDTH].astype(F32) * factor
-    last = sums[8 * WIDTH : 8 * WIDTH + 8].astype(F32) * factor
+                i = 2 * t + n
+                block = moved(block_of(tiles, i), FIRST[i], 0)
+                ref[t, n] = block[:, :WIDTH] * factor
+    last = sums[6 * eighth].astype(F32) * factor
     for t in range(2):
         bias_out[t] = last[2 * t : 2 * t + 2, :WIDTH]
     store.wait()
@@ -510,16 +507,15 @@
 def local(sizes, tokens, cotangent, first_weight, first_bias, second_weight, relu_mask, shrink_mask):
     devices = math.prod(sizes)
     nlat = 2 * devices
-    blocks = 8 * WIDTH // 8 + 1
+    blocks = 6 * WIDTH // 8 + 1
     per_owner = -(-blocks // devices)
     owners = -(-blocks // per_owner)
 
+    pairs = Layout(major_to_minor=(0, 2, 1, 3))
+
     def in_rows(field):
-        return (
-            field.reshape(2, 2, 3 * GROUPS, LANES)
-            .transpose(0, 2, 1, 3)
-            .reshape(2, 6 * GROUPS, LANES)
-        )
+        tiles = with_layout_constraint(field.reshape(2, 2, 3 * GROUPS, LANES), pairs)
+        return tiles.transpose(0, 2, 1, 3).reshape(2, 6 * GROUPS, LANES)
 
     def mask_rows(mask):
         width = mask.shape[-1] // LANES
@@ -534,16 +530,14 @@
     def vmem(*shape, dtype=BF16):
         return pltpu.VMEM(shape, dtype)
 
-    out, first, bias, second = pl.pallas_call(
+    ahead, sums = pl.pallas_call(
         functools.partial(kernel, sizes, per_owner, owners),
         out_shape=(
             jax.ShapeDtypeStruct((2, 6 * GROUPS, LANES), BF16),
-            jax.ShapeDtypeStruct(first_weight.shape, F32),
-            jax.ShapeDtypeStruct(first_bias.shape, F32),
-            jax.ShapeDtypeStruct(second_weight.shape, F32),
+            jax.ShapeDtypeStruct((owners, per_owner, 8, LANES), BF16),
         ),
         in_specs=[anywhere] * 11,
-        out_specs=(anywhere, in_vmem, in_vmem, in_vmem),
+        out_specs=(in_vmem, in_vmem),
         scratch_shapes=[
             vmem(2, 2, 6 * GROUPS, LANES),
             vmem(4, 6 * ROWS, LANES, dtype=F32),
@@ -567,7 +561,6 @@
             vmem(devices, 4, 384),
             vmem(4 * devices, 384),
             vmem(devices, per_owner, 8, LANES),
-            vmem(owners, per_owner, 8, LANES),
             vmem(owners * per_owner, 8, LANES),
             vmem(2, 6 * ROWS, LANES, dtype=F32),
             vmem(4, 2, ROWS, LANES, dtype=F32),
@@ -582,10 +575,9 @@
             pltpu.SemaphoreType.DMA((2,)),
             pltpu.SemaphoreType.DMA((4,)),
             pltpu.SemaphoreType.DMA((4,)),
-            pltpu.SemaphoreType.REGULAR,
         ],
         compiler_params=pltpu.CompilerParams(
-            collective_id=0, has_side_effects=True, vmem_limit_bytes=48 * 1024 * 1024
+            collective_id=0, has_side_effects=True, vmem_limit_bytes=60 * 1024 * 1024
         ),
     )(
         in_rows(tokens),
@@ -597,9 +589,20 @@
         mask_rows(shrink_mask),
         *constants,
     )
-    token_gradient = (
-        out.reshape(2, 3 * GROUPS, 2, LANES).transpose(0, 2, 1, 3).reshape(tokens.shape)
-    )
+    out, first, bias, second = pl.pallas_call(
+        functools.partial(finish, 1.0 / math.sqrt(nlat * 2 * devices)),
+        out_shape=(
+            jax.ShapeDtypeStruct((2, 6 * GROUPS, LANES), BF16),
+            jax.ShapeDtypeStruct(first_weight.shape, F32),
+            jax.ShapeDtypeStruct(first_bias.shape, F32),
+            jax.ShapeDtypeStruct(second_weight.shape, F32),
+        ),
+        in_specs=(in_vmem, in_vmem),
+        out_specs=(anywhere, in_vmem, in_vmem, in_vmem),
+        scratch_shapes=[pltpu.SemaphoreType.DMA],
+    )(ahead, sums.reshape(owners * per_owner, 8, LANES))
+    out = out.reshape(2, 3 * GROUPS, 2, LANES).transpose(0, 2, 1, 3)
+    token_gradient = with_layout_constraint(out, pairs).reshape(tokens.shape)
     return (token_gradient, first, bias, second)
 
 

time: 85.6 us -> 72.4 us (0.85)
  the two profiles are of different devices: /device:TPU:64 before, /device:TPU:8 now
where the time goes in v2:
time: 72.4 us; the launch traced here: 72.3 us
  Pallas kernels  71.6 us (99%)
    pallas_call x1, Pallas kernels, local(): pl.pallas_call(functools.partial(kernel, sizes, per_owner, owners), out_s...  69 us
    pallas_call x1, Pallas kernels, local(): pl.pallas_call(functools.partial(finish, 1.0 / math.sqrt(nlat * 2 * devic...  2.63 us

profile of v2, /device:TPU:8, one launch (start us, length us, event | category | flops | bytes accessed | tf_op | source)
XLA Modules:
  0.0 72.3 jit_solution(16120887967234565193)
XLA Ops:
  0.6 69.0 %shard_map.138 = (bf16[2,1080,128]{2,1,0:T(8,128)(2,1)}, bf16[73,1,8,128]{3,2,1,0:T(8,128)(2,1)}) custom-call(bf16[2,1080,128]{2,1,0:T(8,128)(2,1)} %bitcast.28, bf16[2,1080,128]{2,1,0:T(8,128)(2,1)} %bitcast.29, bf16[2,2,96,96]{3,2,1,0:T(8,128)(2,1)} %w_one.1, bf16[2,2,96]{2,1,0:T(2,128)(2,1)} %b_one.1, bf16[2,2,96,96]{3,2,1,0:T(8,128)(2,1)} %w_two.1, ...), custom_call_target="tpu_custom_call" | custom-call | tf_op jit(solution)/shard_map/pallas_call | solution.py:533
  69.6 2.6 %shard_map.139 = (bf16[2,1080,128]{2,1,0:T(8,128)(2,1)}, f32[2,2,96,96]{3,2,1,0:T(8,128)}, f32[2,2,96]{2,1,0:T(2,128)}, f32[2,2,96,96]{3,2,1,0:T(8,128)}) custom-call(bf16[2,1080,128]{2,1,0:T(8,128)(2,1)} %get-tuple-element.10.ahead, bf16[73,8,128]{2,1,0:T(8,128)(2,1)} %bitcast.30), custom_call_target="tpu_custom_call" | custom-call | tf_op jit(solution)/shard_map/pallas_call | solution.py:592

commit v3 on v2

--- a/solution.py
+++ b/solution.py
@@ -16,6 +16,7 @@
 NAMES = ("lat_0", "lat_1", "lat_2")
 WIDTH = 96
 LANES = 128
+STEP = 7
 ROWS = 192
 GROUPS = 180
 F32 = jnp.float32
@@ -150,6 +151,7 @@
     quarter = nlat // 4
     cx, cz, cy = (lax.axis_index(n) for n in NAMES)
     me = (cx * nz + cz) * ny + cy
+    mine = lax.rem(me * pow(STEP, -1, devices), devices)
 
     def whom(x, z, y):
         return dict(zip(NAMES, (x, z, y)))
@@ -384,15 +386,18 @@
                 block_of(tiles, 2 + n), FIRST[2 + n], 0
             )
             total = jnp.where(row8 == 2 * t + n, value, total)
+    for spare in range(6 * eighth + 1, owners * per_owner):
+        shared[spare] = jnp.zeros((8, LANES), BF16)
     shared[6 * eighth] = total.astype(BF16)
 
     def to_owner(i, carry):
-        p = lax.rem(me + i, owners)
+        number = lax.rem(me + i, owners)
+        p = lax.rem(number * STEP, devices)
 
         @pl.when(p != me)
         def _():
             pltpu.make_async_remote_copy(
-                shared.at[pl.ds(p * per_owner, per_owner)],
+                shared.at[pl.ds(number * per_owner, per_owner)],
                 own_sums.at[me],
                 send_sem.at[2],
                 recv_sem.at[2],
@@ -427,16 +432,16 @@
             device_id_type=MESH,
         )
 
-    @pl.when(me < owners)
+    @pl.when(mine < owners)
     def _():
-        own_sums[me] = shared[pl.ds(me * per_owner, per_owner)]
+        own_sums[me] = shared[pl.ds(mine * per_owner, per_owner)]
         bytes_of(own_sums.at[pl.ds(0, devices - 1)], 2).wait_recv()
-        all_sums[me] = jnp.sum(own_sums[...].astype(F32), axis=0).astype(BF16)
+        all_sums[mine] = jnp.sum(own_sums[...].astype(F32), axis=0).astype(BF16)
 
         def to_all(i, carry):
             pltpu.make_async_remote_copy(
-                all_sums.at[me],
-                all_sums.at[me],
+                all_sums.at[mine],
+                all_sums.at[mine],
                 send_sem.at[3],
                 recv_sem.at[3],
                 device_id=at_index(lax.rem(me + i, devices)),
@@ -446,6 +451,7 @@
 
         lax.fori_loop(1, devices, to_all, 0)
 
+    stores = [pltpu.make_async_copy(raw.at[0, h], out.at[h], load_sem.at[h]) for h in range(2)]
     loads[10].wait()
     own_back.wait()
     whole_back.wait_recv()
@@ -468,20 +474,24 @@
             for c, v in enumerate(tiles_of([result_out[j, n] for j in range(4)])):
                 result[h, pl.ds(2 * c + n, ROWS, stride=6), :] = v
         done = result[h, pl.ds(0, 6 * GROUPS), :] + raw[1, h].astype(F32)
-        out[h] = done.astype(BF16)
+        raw[0, h] = done.astype(BF16)
+        stores[h].start()
 
     whole_back.wait_send()
 
-    @pl.when(me < owners)
+    @pl.when(mine < owners)
     def _():
         bytes_of(shared.at[pl.ds(0, (owners - 1) * per_owner)], 2).wait_send()
         bytes_of(own_sums.at[pl.ds(0, devices - 1)], 3).wait_send()
         bytes_of(all_sums.at[pl.ds(0, owners - 1)], 3).wait_recv()
 
-    @pl.when(me >= owners)
+    @pl.when(mine >= owners)
     def _():
         bytes_of(shared.at[pl.ds(0, owners * per_owner)], 2).wait_send()
         bytes_of(all_sums.at[pl.ds(0, owners)], 3).wait_recv()
+
+    for c in stores:
+        c.wait()
 
 
 def finish(factor, ahead, sums, out, first_out, bias_out, second_out, sem):
@@ -508,7 +518,7 @@
     devices = math.prod(sizes)
     nlat = 2 * devices
     blocks = 6 * WIDTH // 8 + 1
-    per_owner = -(-blocks // devices)
+    per_owner = max(2, -(-blocks // devices))
     owners = -(-blocks // per_owner)
 
     pairs = Layout(major_to_minor=(0, 2, 1, 3))
@@ -537,7 +547,7 @@
             jax.ShapeDtypeStruct((owners, per_owner, 8, LANES), BF16),
         ),
         in_specs=[anywhere] * 11,
-        out_specs=(in_vmem, in_vmem),
+        out_specs=(anywhere, in_vmem),
         scratch_shapes=[
             vmem(2, 2, 6 * GROUPS, LANES),
             vmem(4, 6 * ROWS, LANES, dtype=F32),
@@ -597,7 +607,7 @@
             jax.ShapeDtypeStruct(first_bias.shape, F32),
             jax.ShapeDtypeStruct(second_weight.shape, F32),
         ),
-        in_specs=(in_vmem, in_vmem),
+        in_specs=(anywhere, in_vmem),
         out_specs=(anywhere, in_vmem, in_vmem, in_vmem),
         scratch_shapes=[pltpu.SemaphoreType.DMA],
     )(ahead, sums.reshape(owners * per_owner, 8, LANES))

time: 72.4 us -> 89.2 us (1.23)
  Pallas kernels: 71.6 us -> 88.5 us
    pallas_call x1, Pallas kernels: 2.63 us -> 19.5 us  [local(): pl.pallas_call(functools.partial(finish, 1.0 / math.sqrt(nlat * 2 * devic...]
where the time goes in v3:
time: 89.2 us; the launch traced here: 89.1 us
  Pallas kernels  88.5 us (99%)
    pallas_call x1, Pallas kernels, local(): pl.pallas_call(functools.partial(kernel, sizes, per_owner, owners), out_s...  68.9 us
    pallas_call x1, Pallas kernels, local(): pl.pallas_call(functools.partial(finish, 1.0 / math.sqrt(nlat * 2 * devic...  19.5 us

profile of v3, /device:TPU:8, one launch (start us, length us, event | category | flops | bytes accessed | tf_op | source)
XLA Modules:
  0.0 89.1 jit_solution(8127130951882848826)
XLA Ops:
  0.6 68.9 %shard_map.138 = (bf16[2,1080,128]{2,1,0:T(8,128)(2,1)}, bf16[37,2,8,128]{3,2,1,0:T(8,128)(2,1)}) custom-call(bf16[2,1080,128]{2,1,0:T(8,128)(2,1)} %bitcast.28, bf16[2,1080,128]{2,1,0:T(8,128)(2,1)} %bitcast.29, bf16[2,2,96,96]{3,2,1,0:T(8,128)(2,1)} %w_one.1, bf16[2,2,96]{2,1,0:T(2,128)(2,1)} %b_one.1, bf16[2,2,96,96]{3,2,1,0:T(8,128)(2,1)} %w_two.1, ...), custom_call_target="tpu_custom_call" | custom-call | tf_op jit(solution)/shard_map/pallas_call | solution.py:543
  69.6 19.5 %shard_map.139 = (bf16[2,1080,128]{2,1,0:T(8,128)(2,1)}, f32[2,2,96,96]{3,2,1,0:T(8,128)}, f32[2,2,96]{2,1,0:T(2,128)}, f32[2,2,96,96]{3,2,1,0:T(8,128)}) custom-call(bf16[2,1080,128]{2,1,0:T(8,128)(2,1)} %get-tuple-element.10.ahead, bf16[74,8,128]{2,1,0:T(8,128)(2,1)} %bitcast.30), custom_call_target="tpu_custom_call" | custom-call | tf_op jit(solution)/shard_map/pallas_call | solution.py:602

commit v4 on v2

--- a/solution.py
+++ b/solution.py
@@ -160,8 +160,16 @@
     barrier = pltpu.get_barrier_semaphore()
 
     def greet(i, carry):
-        d = at_index(lax.rem(me + i, devices))
-        pl.semaphore_signal(barrier, inc=1, device_id=d, device_id_type=MESH)
+        step, j = (i // (nx * ny), lax.rem(i, nx * ny))
+        far = (step + 1) // 2 * (1 - 2 * lax.rem(step, 2))
+        z = lax.rem(cz + nz + nz // 2 + far, nz)
+        x = lax.rem(cx + nx // 2 + j // ny, nx)
+        y = lax.rem(cy + ny // 2 + lax.rem(j, ny), ny)
+
+        @pl.when(i != devices - nx * ny + nx // 2 * ny + ny // 2)
+        def _():
+            pl.semaphore_signal(barrier, inc=1, device_id=whom(x, z, y), device_id_type=MESH)
+
         return carry
 
     loads = [
@@ -182,9 +190,11 @@
             )
         )
     ]
-    for c in loads:
+    for c in loads[:3]:
         c.start()
-    lax.fori_loop(1, devices, greet, 0)
+    lax.fori_loop(0, devices, greet, 0)
+    for c in loads[3:]:
+        c.start()
 
     lane = lane_of((ROWS, LANES))
     for i in range(4):
@@ -446,6 +456,7 @@
 
         lax.fori_loop(1, devices, to_all, 0)
 
+    stores = [pltpu.make_async_copy(raw.at[0, h], out.at[h], load_sem.at[h]) for h in range(2)]
     loads[10].wait()
     own_back.wait()
     whole_back.wait_recv()
@@ -468,7 +479,8 @@
             for c, v in enumerate(tiles_of([result_out[j, n] for j in range(4)])):
                 result[h, pl.ds(2 * c + n, ROWS, stride=6), :] = v
         done = result[h, pl.ds(0, 6 * GROUPS), :] + raw[1, h].astype(F32)
-        out[h] = done.astype(BF16)
+        raw[0, h] = done.astype(BF16)
+        stores[h].start()
 
     whole_back.wait_send()
 
@@ -483,10 +495,18 @@
         bytes_of(shared.at[pl.ds(0, owners * per_owner)], 2).wait_send()
         bytes_of(all_sums.at[pl.ds(0, owners)], 3).wait_recv()
 
-
-def finish(factor, ahead, sums, out, first_out, bias_out, second_out, sem):
-    store = pltpu.make_async_copy(ahead, out, sem)
-    store.start()
+    for c in stores:
+        c.wait()
+
+
+def finish(factor, ahead, sums, out, first_out, bias_out, second_out, held, in_sem, out_sem):
+    fetch = [pltpu.make_async_copy(ahead.at[h], held.at[h], in_sem.at[h]) for h in range(2)]
+    store = [pltpu.make_async_copy(held.at[h], out.at[h], out_sem.at[h]) for h in range(2)]
+    for c in fetch:
+        c.start()
+    for h in range(2):
+        fetch[h].wait()
+        store[h].start()
     eighth = WIDTH // 8
     for g, ref in enumerate((first_out, second_out)):
         tiles = [
@@ -501,7 +521,8 @@
     last = sums[6 * eighth].astype(F32) * factor
     for t in range(2):
         bias_out[t] = last[2 * t : 2 * t + 2, :WIDTH]
-    store.wait()
+    for c in store:
+        c.wait()
 
 
 def local(sizes, tokens, cotangent, first_weight, first_bias, second_weight, relu_mask, shrink_mask):
@@ -537,7 +558,7 @@
             jax.ShapeDtypeStruct((owners, per_owner, 8, LANES), BF16),
         ),
         in_specs=[anywhere] * 11,
-        out_specs=(in_vmem, in_vmem),
+        out_specs=(anywhere, in_vmem),
         scratch_shapes=[
             vmem(2, 2, 6 * GROUPS, LANES),
             vmem(4, 6 * ROWS, LANES, dtype=F32),
@@ -597,9 +618,13 @@
             jax.ShapeDtypeStruct(first_bias.shape, F32),
             jax.ShapeDtypeStruct(second_weight.shape, F32),
         ),
-        in_specs=(in_vmem, in_vmem),
+        in_specs=(anywhere, in_vmem),
         out_specs=(anywhere, in_vmem, in_vmem, in_vmem),
-        scratch_shapes=[pltpu.SemaphoreType.DMA],
+        scratch_shapes=[
+            vmem(2, 6 * GROUPS, LANES),
+            pltpu.SemaphoreType.DMA((2,)),
+            pltpu.SemaphoreType.DMA((2,)),
+        ],
     )(ahead, sums.reshape(owners * per_owner, 8, LANES))
     out = out.reshape(2, 3 * GROUPS, 2, LANES).transpose(0, 2, 1, 3)
     token_gradient = with_layout_constraint(out, pairs).reshape(tokens.shape)

time: 72.4 us -> 72.7 us (level)
    pallas_call x1, Pallas kernels: 2.63 us -> 3.44 us  [local(): pl.pallas_call(functools.partial(finish, 1.0 / math.sqrt(nlat * 2 * devic...]
where the time goes in v4:
time: 72.7 us; the launch traced here: 72.5 us
  Pallas kernels  71.9 us (99%)
    pallas_call x1, Pallas kernels, local(): pl.pallas_call(functools.partial(kernel, sizes, per_owner, owners), out_s...  68.4 us
    pallas_call x1, Pallas kernels, local(): pl.pallas_call(functools.partial(finish, 1.0 / math.sqrt(nlat * 2 * devic...  3.44 us

profile of v4, /device:TPU:8, one launch (start us, length us, event | category | flops | bytes accessed | tf_op | source)
XLA Modules:
  0.0 72.5 jit_solution(3001086919517070302)
XLA Ops:
  0.6 68.4 %shard_map.138 = (bf16[2,1080,128]{2,1,0:T(8,128)(2,1)}, bf16[73,1,8,128]{3,2,1,0:T(8,128)(2,1)}) custom-call(bf16[2,1080,128]{2,1,0:T(8,128)(2,1)} %bitcast.28, bf16[2,1080,128]{2,1,0:T(8,128)(2,1)} %bitcast.29, bf16[2,2,96,96]{3,2,1,0:T(8,128)(2,1)} %w_one.1, bf16[2,2,96]{2,1,0:T(2,128)(2,1)} %b_one.1, bf16[2,2,96,96]{3,2,1,0:T(8,128)(2,1)} %w_two.1, ...), custom_call_target="tpu_custom_call" | custom-call | tf_op jit(solution)/shard_map/pallas_call | solution.py:554
  69.1 3.4 %shard_map.139 = (bf16[2,1080,128]{2,1,0:T(8,128)(2,1)}, f32[2,2,96,96]{3,2,1,0:T(8,128)}, f32[2,2,96]{2,1,0:T(2,128)}, f32[2,2,96,96]{3,2,1,0:T(8,128)}) custom-call(bf16[2,1080,128]{2,1,0:T(8,128)(2,1)} %get-tuple-element.10.ahead, bf16[73,8,128]{2,1,0:T(8,128)(2,1)} %bitcast.30), custom_call_target="tpu_custom_call" | custom-call | tf_op jit(solution)/shard_map/pallas_call | solution.py:613

commit v5 on v4

--- a/solution.py
+++ b/solution.py
@@ -146,6 +146,7 @@
 ):
     nx, nz, ny = sizes
     devices = nx * nz * ny
+    assert all(n & (n - 1) == 0 for n in sizes)
     nlat = 2 * devices
     quarter = nlat // 4
     cx, cz, cy = (lax.axis_index(n) for n in NAMES)
@@ -155,21 +156,15 @@
         return dict(zip(NAMES, (x, z, y)))
 
     def at_index(p):
-        return whom(p // (nz * ny), lax.rem(p // ny, nz), lax.rem(p, ny))
+        zy = lax.shift_right_logical(p, ny.bit_length() - 1)
+        x = lax.shift_right_logical(zy, nz.bit_length() - 1)
+        return whom(x, lax.bitwise_and(zy, nz - 1), lax.bitwise_and(p, ny - 1))
 
     barrier = pltpu.get_barrier_semaphore()
 
     def greet(i, carry):
-        step, j = (i // (nx * ny), lax.rem(i, nx * ny))
-        far = (step + 1) // 2 * (1 - 2 * lax.rem(step, 2))
-        z = lax.rem(cz + nz + nz // 2 + far, nz)
-        x = lax.rem(cx + nx // 2 + j // ny, nx)
-        y = lax.rem(cy + ny // 2 + lax.rem(j, ny), ny)
-
-        @pl.when(i != devices - nx * ny + nx // 2 * ny + ny // 2)
-        def _():
-            pl.semaphore_signal(barrier, inc=1, device_id=whom(x, z, y), device_id_type=MESH)
-
+        d = at_index(lax.bitwise_and(me + i, devices - 1))
+        pl.semaphore_signal(barrier, inc=1, device_id=d, device_id_type=MESH)
         return carry
 
     loads = [
@@ -190,11 +185,9 @@
             )
         )
     ]
-    for c in loads[:3]:
+    for c in loads:
         c.start()
-    lax.fori_loop(0, devices, greet, 0)
-    for c in loads[3:]:
-        c.start()
+    lax.fori_loop(1, devices, greet, 0)
 
     lane = lane_of((ROWS, LANES))
     for i in range(4):
@@ -242,7 +235,7 @@
 
     def exchange(src, dst, n):
         def send(i, carry):
-            p = lax.rem(me + i, devices)
+            p = lax.bitwise_and(me + i, devices - 1)
             pltpu.make_async_remote_copy(
                 src.at[pl.ds(p, 1)],
                 dst.at[pl.ds(me, 1)],
@@ -449,7 +442,7 @@
                 all_sums.at[me],
                 send_sem.at[3],
                 recv_sem.at[3],
-                device_id=at_index(lax.rem(me + i, devices)),
+                device_id=at_index(lax.bitwise_and(me + i, devices - 1)),
                 device_id_type=MESH,
             ).start()
             return carry
@@ -499,16 +492,37 @@
         c.wait()
 
 
-def finish(factor, ahead, sums, out, first_out, bias_out, second_out, held, in_sem, out_sem):
-    fetch = [pltpu.make_async_copy(ahead.at[h], held.at[h], in_sem.at[h]) for h in range(2)]
-    store = [pltpu.make_async_copy(held.at[h], out.at[h], out_sem.at[h]) for h in range(2)]
+def finish(
+    factor,
+    ahead,
+    sums_in,
+    out,
+    first_out,
+    bias_out,
+    second_out,
+    held,
+    sums,
+    first_v,
+    bias_v,
+    second_v,
+    in_sem,
+    out_sem,
+):
+    fetch = [
+        pltpu.make_async_copy(src, dst, in_sem.at[i])
+        for i, (src, dst) in enumerate(((ahead, held), (sums_in, sums)))
+    ]
+    store = [
+        pltpu.make_async_copy(src, dst, out_sem.at[i])
+        for i, (src, dst) in enumerate(
+            ((held, out), (first_v, first_out), (second_v, second_out), (bias_v, bias_out))
+        )
+    ]
     for c in fetch:
         c.start()
-    for h in range(2):
-        fetch[h].wait()
-        store[h].start()
+    fetch[1].wait()
     eighth = WIDTH // 8
-    for g, ref in enumerate((first_out, second_out)):
+    for g, ref in enumerate((first_v, second_v)):
         tiles = [
             sums[pl.ds((3 * g + c) * eighth, eighth)].reshape(WIDTH, LANES).astype(F32)
             for c in range(3)
@@ -518,9 +532,14 @@
                 i = 2 * t + n
                 block = moved(block_of(tiles, i), FIRST[i], 0)
                 ref[t, n] = block[:, :WIDTH] * factor
+        if g == 0:
+            fetch[0].wait()
+            store[0].start()
+        store[1 + g].start()
     last = sums[6 * eighth].astype(F32) * factor
     for t in range(2):
-        bias_out[t] = last[2 * t : 2 * t + 2, :WIDTH]
+        bias_v[t] = last[2 * t : 2 * t + 2, :WIDTH]
+    store[3].start()
     for c in store:
         c.wait()
 
@@ -618,12 +637,16 @@
             jax.ShapeDtypeStruct(first_bias.shape, F32),
             jax.ShapeDtypeStruct(second_weight.shape, F32),
         ),
-        in_specs=(anywhere, in_vmem),
-        out_specs=(anywhere, in_vmem, in_vmem, in_vmem),
+        in_specs=(anywhere, anywhere),
+        out_specs=(anywhere,) * 4,
         scratch_shapes=[
             vmem(2, 6 * GROUPS, LANES),
+            vmem(owners * per_owner, 8, LANES),
+            vmem(*first_weight.shape, dtype=F32),
+            vmem(*first_bias.shape, dtype=F32),
+            vmem(*second_weight.shape, dtype=F32),
             pltpu.SemaphoreType.DMA((2,)),
-            pltpu.SemaphoreType.DMA((2,)),
+            pltpu.SemaphoreType.DMA((4,)),
         ],
     )(ahead, sums.reshape(owners * per_owner, 8, LANES))
     out = out.reshape(2, 3 * GROUPS, 2, LANES).transpose(0, 2, 1, 3)

time: 72.7 us -> 69.1 us (0.950)
  Pallas kernels: 71.9 us -> 68.3 us
    pallas_call x1, Pallas kernels: 68.4 us -> 66.2 us  [local(): pl.pallas_call(functools.partial(kernel, sizes, per_owner, owners), out_s...]
    pallas_call x1, Pallas kernels: 3.44 us -> 2.15 us  [local(): pl.pallas_call(functools.partial(finish, 1.0 / math.sqrt(nlat * 2 * devic...]
where the time goes in v5:
time: 69.1 us; the launch traced here: 69 us
  Pallas kernels  68.3 us (99%)
    pallas_call x1, Pallas kernels, local(): pl.pallas_call(functools.partial(kernel, sizes, per_owner, owners), out_s...  66.2 us
    pallas_call x1, Pallas kernels, local(): pl.pallas_call(functools.partial(finish, 1.0 / math.sqrt(nlat * 2 * devic...  2.15 us

profile of v5, /device:TPU:8, one launch (start us, length us, event | category | flops | bytes accessed | tf_op | source)
XLA Modules:
  0.0 69.0 jit_solution(9369485276443625454)
XLA Ops:
  0.6 66.2 %shard_map.138 = (bf16[2,1080,128]{2,1,0:T(8,128)(2,1)}, bf16[73,1,8,128]{3,2,1,0:T(8,128)(2,1)}) custom-call(bf16[2,1080,128]{2,1,0:T(8,128)(2,1)} %bitcast.28, bf16[2,1080,128]{2,1,0:T(8,128)(2,1)} %bitcast.29, bf16[2,2,96,96]{3,2,1,0:T(8,128)(2,1)} %w_one.1, bf16[2,2,96]{2,1,0:T(2,128)(2,1)} %b_one.1, bf16[2,2,96,96]{3,2,1,0:T(8,128)(2,1)} %w_two.1, ...), custom_call_target="tpu_custom_call" | custom-call | tf_op jit(solution)/shard_map/pallas_call | solution.py:573
  66.8 2.1 %shard_map.139 = (bf16[2,1080,128]{2,1,0:T(8,128)(2,1)}, f32[2,2,96,96]{3,2,1,0:T(8,128)}, f32[2,2,96]{2,1,0:T(2,128)}, f32[2,2,96,96]{3,2,1,0:T(8,128)}) custom-call(bf16[2,1080,128]{2,1,0:T(8,128)(2,1)} %get-tuple-element.10.ahead, bf16[73,8,128]{2,1,0:T(8,128)(2,1)} %bitcast.30), custom_call_target="tpu_custom_call" | custom-call | tf_op jit(solution)/shard_map/pallas_call | solution.py:632
